TPU v7x, 32 devices: a whole 2x2x4 slice. The times are simulated.
32 devices in a mesh: sta: 2 (over x), gx: 4 (over z), gy: 4 (over y, core).
Axes of the slice: x: 2, y: 2, z: 4, core: 2. Of those that a mesh axis runs over, the one named last changes fastest.
Arguments:
- record: float32 [128, 1024], replicated, may hold values from -6 to 6
- shifts: int32 [128, 256], P(None, 'gx'), may hold values from 0 to 1022
- station_group: int32 [128], replicated, may hold values from 0 to 7
- weights: bfloat16 [128, 256, 512], P('sta', 'gy'), may hold values from -6 to 6
- psf_real: float32 [256, 256, 512], P(None, 'gx', 'gy'), may hold values from -6 to 6
- psf_imag: float32 [256, 256, 512], P(None, 'gx', 'gy'), may hold values from -6 to 6
Outputs:
- image: float32 [2, 256, 256, 512], P('sta', 'gx', 'gy')
All inputs are finite; a program needn't handle non-finite values.
Results may differ from a plain program's by a relative error of at most 0.0029.
Values may be sent and summed in bfloat16 or wider, within the bound.
A program may use at most 128 MiB of HBM per device.

v0:
```python
import math

import jax
import jax.numpy as jnp
from jax import lax
from jax.sharding import PartitionSpec as P

T_DEV = 1
NZ = 256
NX = 256
GROUPS = 8


NOISE_POWER = 0.25
HIGHEST = lax.Precision.HIGHEST


def station_counts(station_group):
    labels = jnp.arange(GROUPS, dtype=jnp.int32)
    onehot = (station_group[:, None] == labels[None, :]).astype(jnp.float32)
    totals = jnp.sum(onehot, axis=0)
    return jnp.dot(onehot, totals, precision=HIGHEST)


def coefficients(record, shifts, per_station, first_time, num_times):
    times_range = first_time + jnp.arange(num_times, dtype=jnp.int32)
    positions = shifts[:, :, None] + times_range[None, None, :]
    values = jnp.take_along_axis(record, positions.reshape(positions.shape[0], -1), axis=1)
    scaled = values.reshape(positions.shape) / per_station[:, None, None]
    return jnp.transpose(scaled, (2, 1, 0)).astype(jnp.bfloat16)


def fourier_parts(length, scale):
    indices = jnp.arange(length, dtype=jnp.int32)
    product = indices[:, None] * indices[None, :] % length
    angles = product.astype(jnp.float32) * (2.0 * math.pi / length)
    return (jnp.cos(angles) * scale, jnp.sin(angles) * scale)


def complex_table(length, forward):
    if forward:
        cosine, sine = fourier_parts(length, 1.0)
        return jnp.stack([jnp.stack([cosine, sine]), jnp.stack([-sine, cosine])])
    cosine, sine = fourier_parts(length, 1.0 / length)
    return jnp.stack([jnp.stack([cosine, -sine]), jnp.stack([sine, cosine])])


def along_rows(piece, table):
    return jnp.einsum("itzny,oikn->otzky", piece, table, precision=HIGHEST)


def along_depth(piece, table):
    return jnp.einsum("itnxy,oikn->otkxy", piece, table, precision=HIGHEST)


def on_device(record, shifts, station_group, weights, psf_real, psf_imag):
    per_station = station_counts(station_group)
    depth_rows = shifts.shape[1]
    lateral_rows = weights.shape[1]
    width_y = weights.shape[2]
    columns = lateral_rows * width_y
    first_time = lax.axis_index("sta") * T_DEV
    coefficient = coefficients(record, shifts, per_station, first_time, T_DEV)
    coefficient = coefficient.reshape(T_DEV * depth_rows, coefficient.shape[2])
    piece = lax.all_gather(weights, "sta", axis=0, tiled=True)
    stack = jnp.dot(
        coefficient, piece.reshape(piece.shape[0], columns), preferred_element_type=jnp.float32
    )
    stack = stack.reshape(T_DEV, depth_rows, lateral_rows, width_y)
    cosine_y, sine_y = fourier_parts(width_y, 1.0)
    spectrum = jnp.einsum(
        "tzxn,okn->otzxk", stack, jnp.stack([cosine_y, -sine_y]), precision=HIGHEST
    )
    row_table = complex_table(NX, True)
    by_rows = along_rows(
        lax.all_to_all(spectrum, "gy", split_axis=4, concat_axis=3, tiled=True), row_table
    )
    depth_table = complex_table(NZ, True)
    by_depth = along_depth(
        lax.all_to_all(by_rows, "gx", split_axis=3, concat_axis=2, tiled=True), depth_table
    )
    power = psf_real * psf_real + psf_imag * psf_imag + NOISE_POWER
    filt_real = (psf_real * by_depth[0] + psf_imag * by_depth[1]) / power
    filt_imag = (psf_real * by_depth[1] - psf_imag * by_depth[0]) / power
    back_depth = along_depth(jnp.stack([filt_real, filt_imag]), complex_table(NZ, False))
    back_table = complex_table(NX, False)
    back_rows = along_rows(
        lax.all_to_all(back_depth, "gx", split_axis=2, concat_axis=3, tiled=True), back_table
    )
    cosine_back, sine_back = fourier_parts(width_y, 1.0 / width_y)
    real_table = jnp.stack([cosine_back, -sine_back])
    return jnp.einsum(
        "itzxk,iyk->tzxy",
        lax.all_to_all(back_rows, "gy", split_axis=3, concat_axis=4, tiled=True),
        real_table,
        precision=HIGHEST,
    )


def solution(mesh):
    in_specs = (
        P(),
        P(None, "gx"),
        P(),
        P("sta", "gy", None),
        P(None, "gx", "gy"),
        P(None, "gx", "gy"),
    )
    out_specs = P("sta", "gx", "gy", None)
    return jax.shard_map(
        on_device, mesh=mesh, in_specs=in_specs, out_specs=out_specs, check_vma=False
    )
```

profile of v0, /device:TPU:0, one launch (start us, length us, event | category | flops | bytes accessed | tf_op | source)
XLA Modules:
  0.0 1795.1 jit_solution(12204414173236753648)
XLA Ops:
  8.2 65.0 %gather_fusion = f32[8192]{0:T(1024)S(1)} fusion(f32[128,1024]{1,0:T(8,128)S(1)} %copy-done, s32[8192]{0:T(1024)S(1)} %reshape.275), kind=kCustom, calls=%fused_computation | custom fusion | bytes 131072 | tf_op jit(solution)/shard_map/jit(take_along_axis)/gather | solution.py:28
  77.7 37.9 %all-gather.2.cloned.1.call-done = bf16[128,64,512]{2,1,0:T(8,128)(2,1)} async-done(((bf16[64,64,512]{2,1,0:T(8,128)(2,1)}), bf16[128,64,512]{2,1,0:T(8,128)(2,1)}) %all-gather.2.cloned.1.call-update) | async-done | bytes 8388624 | tf_op jit(solution)/shard_map/all_gather | solution.py:65
  115.6 13.0 copy.78
  135.1 32.3 %fusion.12 = f32[2,1,64,64,512]{4,3,2,0,1:T(8,128)} fusion(f32[64,64,512]{2,0,1:T(8,128)S(1)} %fusion.3, f32[1,512,512]{2,1,0:T(8,128)S(1)} %get-tuple-element.12, f32[1,512,512]{2,1,0:T(8,128)S(1)} %get-tuple-element.11), kind=kOutput, calls=%fused_computation.22 | convolution fusion | flops 25770328064 | bytes 27262976 | tf_op jit(solution)/shard_map/tzxn,okn->otzxk/dot_general | solution.py:71
  167.4 30.5 %copy.54 = f32[2,1,64,64,512]{3,2,0,1,4:T(8,128)} copy(f32[2,1,64,64,512]{4,3,2,0,1:T(8,128)} %fusion.12) | data formatting | bytes 33554432 | tf_op jit(solution)/shard_map/tzxn,okn->otzxk/transpose | solution.py:71
  198.0 42.3 %reshape.303 = f32[4,1,1048576]{2,1,0:T(1,128)} reshape(f32[512,1,2,64,64]{4,3,2,1,0:T(8,128)} %bitcast.153) | data formatting | bytes 33554432
  249.4 180.9 %all-to-all-done = f32[4,1,1048576]{2,1,0:T(1,128)} async-done(((f32[4,1,1048576]{2,1,0:T(1,128)}), f32[4,1,1048576]{2,1,0:T(1,128)}, u32[]{:S(2)}, u32[]{:S(2)}) %all-to-all-start) | async-done | bytes 16777248 | tf_op jit(solution)/shard_map/all_to_all | solution.py:76
  430.8 54.4 %reduce = f32[4,1048576]{1,0:T(4,128)} reduce(f32[4,1,1048576]{2,1,0:T(1,128)} %all-to-all-done, f32[]{:T(128)} %broadcast.479), dimensions={1}, to_apply=%all_to_all.44.reduce_sub_computation | reduce | bytes 33554436 | tf_op jit(solution)/shard_map/all_to_all | solution.py:76
  485.3 55.1 %reshape.304 = f32[512,1,2,64,64]{4,3,2,1,0:T(8,128)} reshape(f32[4,1048576]{1,0:T(4,128)} %reduce) | data formatting | bytes 33554432
  540.4 24.6 %copy.55 = f32[2,1,64,64,4,128]{5,3,4,0,2,1:T(8,128)} copy(f32[2,1,64,64,4,128]{3,2,0,5,4,1:T(8,128)} %bitcast.154) | data formatting | bytes 33554432 | tf_op jit(solution)/shard_map/all_to_all | solution.py:76
  565.0 31.2 %convolution_bitcast_fusion.2 = f32[2,1,64,256,128]{4,3,2,0,1:T(8,128)S(1)} fusion(f32[2,64,256,128,1]{3,2,0,1,4:T(8,128)} %bitcast.155, f32[1,2,256,256]{3,2,1,0:T(8,128)S(1)} %get-tuple-element.10, f32[1,2,256,256]{3,2,1,0:T(8,128)S(1)} %get-tuple-element.9), kind=kOutput, calls=%fused_computation.26 | convolution fusion | flops 25770065920 | bytes 34603008 | tf_op jit(solution)/shard_map/itzny,oikn->otzky/dot_general | solution.py:49
  596.1 20.0 %copy.56 = f32[2,1,64,256,128]{4,2,0,1,3:T(8,128)} copy(f32[2,1,64,256,128]{4,3,2,0,1:T(8,128)S(1)} %convolution_bitcast_fusion.2) | data formatting | bytes 33554432 | tf_op jit(solution)/shard_map/itzny,oikn->otzky/transpose | solution.py:49
  625.5 360.8 %all-to-all-done.1 = f32[2,1,64,256,128]{4,2,0,1,3:T(8,128)} async-done(((f32[2,1,64,256,128]{4,2,0,1,3:T(8,128)}), f32[2,1,64,256,128]{4,2,0,1,3:T(8,128)}, u32[]{:S(2)}, u32[]{:S(2)}) %all-to-all-start.1) | async-done | bytes 16777248 | tf_op jit(solution)/shard_map/all_to_all | solution.py:80
  992.8 31.0 %convolution_bitcast_fusion.1 = f32[2,256,64,128]{3,1,2,0:T(8,128)} fusion(f32[2,256,64,128,1]{3,1,0,2,4:T(8,128)S(1)} %bitcast.156, f32[1,2,256,256]{3,2,1,0:T(8,128)S(1)} %get-tuple-element.10, f32[1,2,256,256]{3,2,1,0:T(8,128)S(1)} %get-tuple-element.9), kind=kOutput, calls=%fused_computation.25 | convolution fusion | flops 25770065920 | bytes 34603008 | tf_op jit(solution)/shard_map/itnxy,oikn->otkxy/dot_general | solution.py:53
  1023.8 22.4 %fusion.5 = (f32[1,1,256,64,128]{4,2,3,1,0:T(8,128)}, f32[1,1,256,64,128]{4,2,3,1,0:T(8,128)}) fusion(f32[2,256,64,128]{3,1,2,0:T(8,128)} %convolution_bitcast_fusion.1, f32[256,64,128]{2,1,0:T(8,128)} %param.11, f32[256,64,128]{2,1,0:T(8,128)} %param.10), kind=kLoop, calls=%fused_computation.10 | loop fusion | flops 25165824 | bytes 50331648 | tf_op jit(solution)/shard_map/stack | solution.py:85
  1046.2 31.2 %fusion.15 = f32[2,1,256,64,128]{4,2,3,0,1:T(8,128)S(1)} fusion(f32[1,2,256,256]{3,2,1,0:T(8,128)S(1)} %get-tuple-element.8, f32[1,2,256,256]{3,2,1,0:T(8,128)S(1)} %get-tuple-element.7, f32[1,1,256,64,128]{4,2,3,1,0:T(8,128)} %get-tuple-element.6, f32[1,1,256,64,128]{4,2,3,1,0:T(8,128)} %get-tuple-element.5), kind=kOutput, calls=%fused_computation.23 | convolution fusion | flops 25774260224 | bytes 34603008 | tf_op jit(solution)/shard_map/itnxy,oikn->otkxy/dot_general | solution.py:53
  1077.4 20.0 %copy.64 = f32[2,1,256,64,128]{4,3,0,1,2:T(8,128)} copy(f32[2,1,256,64,128]{4,2,3,0,1:T(8,128)S(1)} %fusion.15) | data formatting | bytes 33554432 | tf_op jit(solution)/shard_map/itnxy,oikn->otkxy/transpose | solution.py:53
  1097.4 373.6 %all_to_all.60 = f32[2,1,256,64,128]{4,3,0,1,2:T(8,128)} all-to-all(f32[2,1,256,64,128]{4,3,0,1,2:T(8,128)} %copy.64), channel_id=1, replica_groups=mesh['sta'=2,'gx'=4,'gy'=4] {'gx'}, dimensions={2} | all-to-all | bytes 33554432 | tf_op jit(solution)/shard_map/all_to_all | solution.py:88
  1477.6 31.0 %convolution_bitcast_fusion = f32[2,1,64,256,128]{4,3,2,0,1:T(8,128)} fusion(f32[2,64,256,128,1]{3,2,0,1,4:T(8,128)S(1)} %bitcast.157, f32[1,2,256,256]{3,2,1,0:T(8,128)S(1)} %get-tuple-element.8, f32[1,2,256,256]{3,2,1,0:T(8,128)S(1)} %get-tuple-element.7), kind=kOutput, calls=%fused_computation.24 | convolution fusion | flops 25770065920 | bytes 34603008 | tf_op jit(solution)/shard_map/itzny,oikn->otzky/dot_general | solution.py:49
  1508.6 17.7 copy.66
  1537.6 178.9 %all-to-all-done.3 = f32[2,1,64,256,128]{4,2,0,1,3:T(8,128)} async-done(((f32[2,1,64,256,128]{4,2,0,1,3:T(8,128)}), f32[2,1,64,256,128]{4,2,0,1,3:T(8,128)}, u32[]{:S(2)}, u32[]{:S(2)}) %all-to-all-start.3) | async-done | bytes 16777248 | tf_op jit(solution)/shard_map/all_to_all | solution.py:94
  1716.5 20.8 %copy.96 = f32[2,1,64,4,64,128]{5,3,4,0,2,1:T(4,128)} copy(f32[2,1,64,4,64,128]{5,2,0,4,3,1:T(8,128)} %bitcast.57) | data formatting | bytes 33554432 | tf_op jit(solution)/shard_map/all_to_all | solution.py:94
  1737.4 19.9 %reshape.274 = f32[2,64,64,512]{3,2,0,1:T(8,128)} reshape(f32[2,1,64,64,4,128]{5,4,3,0,2,1:T(4,128)} %bitcast.159) | data formatting | bytes 33554432 | tf_op jit(solution)/shard_map/reshape.27
  1757.2 30.7 %convolution_bitcast_fusion.3 = f32[1,64,64,512]{3,2,1,0:T(8,128)} fusion(f32[2,64,64,512]{3,2,0,1:T(8,128)} %reshape.274, f32[1,512,512]{2,1,0:T(8,128)S(1)} %get-tuple-element.17, f32[1,512,512]{2,1,0:T(8,128)S(1)} %get-tuple-element.18), kind=kOutput, calls=%fused_computation.27 | convolution fusion | flops 25770328064 | bytes 27262976 | tf_op jit(solution)/shard_map/itzxk,iyk->tzxy/dot_general | solution.py:92
  (29 shorter events, 55.9 us)
Async XLA Ops:
  6.5 1.7 copy-start
  6.5 109.1 %all-gather.2.cloned.1.call-start = ((), (), s32[]{:S(2)}) async-start(), calls=%async_computation.4 | async-start | bytes 12582912 | tf_op jit(solution)/shard_map/all_gather | solution.py:65
  8.2 65.1 %copy-start.2 = (s32[128]{0:T(128)S(1)}, s32[128]{0:T(128)}, u32[]{:S(2)}) copy-start(s32[128]{0:T(128)} %param.8) | copy-start | bytes 1540
  240.3 190.0 %all-to-all-start = ((f32[4,1,1048576]{2,1,0:T(1,128)}), f32[4,1,1048576]{2,1,0:T(1,128)}, u32[]{:S(2)}, u32[]{:S(2)}) async-start(f32[4,1,1048576]{2,1,0:T(1,128)} %reshape.303), calls=%async_computation | async-start | bytes 33554432 | tf_op jit(solution)/shard_map/all_to_all | solution.py:76
  616.2 370.1 %all-to-all-start.1 = ((f32[2,1,64,256,128]{4,2,0,1,3:T(8,128)}), f32[2,1,64,256,128]{4,2,0,1,3:T(8,128)}, u32[]{:S(2)}, u32[]{:S(2)}) async-start(f32[2,1,64,256,128]{4,2,0,1,3:T(8,128)} %copy.56), calls=%async_computation.1 | async-start | bytes 33554432 | tf_op jit(solution)/shard_map/all_to_all | solution.py:80
  1526.3 190.2 %all-to-all-start.3 = ((f32[2,1,64,256,128]{4,2,0,1,3:T(8,128)}), f32[2,1,64,256,128]{4,2,0,1,3:T(8,128)}, u32[]{:S(2)}, u32[]{:S(2)}) async-start(f32[2,1,64,256,128]{4,2,0,1,3:T(8,128)} %copy.66), calls=%async_computation.3 | async-start | bytes 33554432 | tf_op jit(solution)/shard_map/all_to_all | solution.py:94
  1757.2 30.7 %copy-start.1 = (f32[128,1024]{1,0:T(8,128)S(1)}, f32[128,1024]{1,0:T(8,128)}, u32[]{:S(2)}) copy-start(f32[128,1024]{1,0:T(8,128)} %param.6) | copy-start | bytes 1572868
Sparse Core Ops, SparseCore 0:
  8.9 106.6 all-gather.1
where the time goes:
time: 1800 us
  waiting for transfers between devices  759 us (42%)
  blocking collectives  374 us (21%)
  local copies, waits for them, and re-layouts  344 us (19%)
  matrix products  194 us (11%)
  other arithmetic  89.5 us (5%)
  starting transfers between devices  21.3 us (1%)
    all_to_all x1, blocking collectives, on_device(): lax.all_to_all(back_depth, 'gx', split_axis=2, concat_axis=3, tiled=True)  374 us
    all_to_all x1, waiting for transfers between devices, on_device(): lax.all_to_all(by_rows, 'gx', split_axis=3, concat_axis=2, tiled=True)  361 us
    all_to_all x1, waiting for transfers between devices, on_device(): lax.all_to_all(spectrum, 'gy', split_axis=4, concat_axis=3, tiled=True)  181 us
    all_to_all x1, waiting for transfers between devices, on_device(): lax.all_to_all(back_rows, 'gy', split_axis=3, concat_axis=4, tiled=True)  179 us
    unnamed x9, local copies, waits for them, and re-layouts  98.3 us
    gather x3, local copies, waits for them, and re-layouts, coefficients(): jnp.take_along_axis(record, positions.reshape(positions.shape[0], -1), ax...  65.1 us
    dot_general x2, matrix products, along_depth(): return jnp.einsum('itnxy,oikn->otkxy', piece, table, precision=HIGHEST)  62.2 us
    dot_general x2, matrix products, along_rows(): return jnp.einsum('itzny,oikn->otzky', piece, table, precision=HIGHEST)  62.1 us
  transfers between devices with their start and end apart: 4, of which 4 were waited for; matrix products, arithmetic and copies ran while one was open for 4% of the time, Pallas kernels for 0%

commit v1 on v0

v1 whole, which is shorter than its diff:
```python
import functools
import math

import jax
import jax.numpy as jnp
from jax import lax
from jax.experimental import pallas as pl
from jax.experimental.pallas import tpu as pltpu
from jax.sharding import PartitionSpec as P

GROUPS = 8
NOISE_POWER = 0.25
HIGHEST = lax.Precision.HIGHEST
VMEM_BYTES = 50 * 1024 * 1024
BLOCK = 16


def station_counts(station_group):
    labels = jnp.arange(GROUPS, dtype=jnp.int32)
    onehot = (station_group[:, None] == labels[None, :]).astype(jnp.float32)
    totals = jnp.sum(onehot, axis=0)
    return jnp.dot(onehot, totals, precision=HIGHEST)


def coefficients(record, shifts, per_station, time):
    positions = shifts + time
    samples = jnp.arange(record.shape[1], dtype=jnp.int32)
    chosen = jnp.where(
        positions[:, :, None] == samples[None, None, :], record[:, None, :], 0.0
    )
    values = jnp.sum(chosen, axis=2)
    scaled = values / per_station[:, None]
    return jnp.transpose(scaled, (1, 0)).astype(jnp.bfloat16)


def fourier_parts(rows, columns, length, scale):
    angles = (rows[:, None] * columns[None, :] % length).astype(jnp.float32)
    angles = angles * (2.0 * math.pi / length)
    return jnp.cos(angles) * scale, jnp.sin(angles) * scale


def halves(table):
    high = lax.reduce_precision(table, 8, 7)
    return high.astype(jnp.bfloat16), (table - high).astype(jnp.bfloat16)


def dot(a, b):
    return jnp.dot(a, b, preferred_element_type=jnp.float32)


def dot3(high, low, value):
    value_high = value.astype(jnp.bfloat16)
    value_low = (value - value_high.astype(jnp.float32)).astype(jnp.bfloat16)
    return dot(high, value_high) + dot(low, value_high) + dot(high, value_low)


def cost(flops, arrays):
    moved = sum(math.prod(a.shape) * jnp.dtype(a.dtype).itemsize for a in arrays)
    return pl.CostEstimate(flops=flops, bytes_accessed=moved, transcendentals=0)


def whole(array):
    rank = len(array.shape)
    return pl.BlockSpec(array.shape, lambda i: (0,) * rank)


PARAMS = pltpu.CompilerParams(vmem_limit_bytes=VMEM_BYTES)


def lateral_kernel(weights, y_high, y_low, x_high, x_low, out, rest, held):
    parts, stations, rows, width = weights.shape
    bins = out.shape[0]
    half = out.shape[2] // 2
    for s in range(stations):
        piece = weights[:, s, :, :].reshape(parts * rows, width)
        along_y = dot(piece, y_high[...]) + dot(piece, y_low[...])
        both = dot3(x_high[...], x_low[...], along_y)
        cosine, sine = both[:bins], both[bins:]
        held[:, s, :half] = cosine[:, :half] + sine[:, half:]
        held[:, s, half:] = cosine[:, half:] - sine[:, :half]
    value = held[...]
    high = value.astype(out.dtype)
    out[...] = high
    rest[...] = (value - high.astype(jnp.float32)).astype(rest.dtype)


def lateral(weights, y_parts, x_parts):
    parts, stations, rows, width = weights.shape
    bins = x_parts[0].shape[0] // 2
    columns = y_parts[0].shape[1]
    tables = [*y_parts, *x_parts]
    result = jax.ShapeDtypeStruct((bins, stations, columns), jnp.bfloat16)
    spec = pl.BlockSpec((bins, BLOCK, columns), lambda i: (0, i, 0))
    macs = stations * parts * rows * columns * (2 * width + 6 * bins)
    return pl.pallas_call(
        lateral_kernel,
        grid=(stations // BLOCK,),
        in_specs=[
            pl.BlockSpec((parts, BLOCK, rows, width), lambda i: (0, i, 0, 0)),
            *[whole(t) for t in tables],
        ],
        out_specs=[spec, spec],
        out_shape=[result, result],
        scratch_shapes=[pltpu.VMEM((bins, BLOCK, columns), jnp.float32)],
        compiler_params=PARAMS,
        cost_estimate=cost(4 * macs, [weights, result, result]),
        name="lateral",
    )(weights, *tables)


def depth_kernel(pieces, outs, coef, *refs):
    spectra = refs[:pieces]
    psf_real, psf_imag, z_high, z_low = refs[pieces : pieces + 4]
    out_refs, held = refs[pieces + 4 : -1], refs[-1]
    depth, block, half = psf_real.shape
    main = 2 * pieces // 3
    coef_whole = coef[...]
    for b in range(block):
        piece = jnp.concatenate([r[b] for r in spectra[:main]], axis=0)
        rest = jnp.concatenate([r[b] for r in spectra[main:]], axis=0)
        rows = 2 * piece.shape[0]
        both = dot(coef_whole[:, :rows], jnp.concatenate([piece, piece], axis=0))
        both = both + dot(coef_whole[:, rows:], rest)
        real_part, imag_part = both[:depth], both[depth:]
        spec_real = real_part[:, :half] - imag_part[:, half:]
        spec_imag = real_part[:, half:] + imag_part[:, :half]
        p_real, p_imag = psf_real[:, b, :], psf_imag[:, b, :]
        inverse = 1.0 / (p_real * p_real + p_imag * p_imag + NOISE_POWER)
        filt_real = (p_real * spec_real + p_imag * spec_imag) * inverse
        filt_imag = (p_real * spec_imag - p_imag * spec_real) * inverse
        filtered = jnp.concatenate([filt_real, filt_imag], axis=1)
        back = dot3(z_high[...], z_low[...], filtered)
        cosine, sine = back[:depth], back[depth:]
        held[:, b, :half] = cosine[:, :half] - sine[:, half:]
        held[:, b, half:] = cosine[:, half:] + sine[:, :half]
    size = depth // outs
    for k in range(outs):
        out_refs[k][...] = held[k * size : (k + 1) * size].astype(out_refs[k].dtype)


def depth_stage(coef, spectra, psf_real, psf_imag, z_parts, outs, first, bins):
    _, stations, columns = spectra[0].shape
    depth, _, width = psf_real.shape
    block = min(BLOCK, bins)
    skip = first // block
    size = depth // outs
    result = jax.ShapeDtypeStruct((size, bins, columns), jnp.bfloat16)
    psf_spec = pl.BlockSpec((depth, block, width), lambda i: (0, i + skip, 0))
    field = jax.ShapeDtypeStruct((depth, bins, columns), jnp.float32)
    macs = 2 * depth * bins * columns * (coef.shape[1] + 3 * depth)
    return pl.pallas_call(
        functools.partial(depth_kernel, len(spectra), outs),
        grid=(bins // block,),
        in_specs=[
            whole(coef),
            *[
                pl.BlockSpec((block, stations, columns), lambda i: (i + skip, 0, 0))
                for _ in spectra
            ],
            psf_spec,
            psf_spec,
            *[whole(t) for t in z_parts],
        ],
        out_specs=[pl.BlockSpec((size, block, columns), lambda i: (0, i, 0))] * outs,
        out_shape=[result] * outs,
        scratch_shapes=[pltpu.VMEM((depth, block, columns), jnp.float32)],
        compiler_params=PARAMS,
        cost_estimate=cost(4 * macs, [field, field]),
        name="depth",
    )(coef, *spectra, psf_real, psf_imag, *z_parts)


def rows_kernel(pieces, *refs):
    field, (x_high, x_low), outs = refs[:pieces], refs[pieces : pieces + 2], refs[pieces + 2 :]
    block, _, columns = field[0].shape
    half = columns // 2
    length = x_high.shape[1]
    size = length // len(outs)
    for z in range(block):
        piece = jnp.concatenate([f[z] for f in field], axis=0)
        both = dot(x_high[...], piece) + dot(x_low[...], piece)
        cosine, sine = both[:length], both[length:]
        back = jnp.concatenate(
            [cosine[:, :half] - sine[:, half:], cosine[:, half:] + sine[:, :half]], axis=1
        ).astype(jnp.bfloat16)
        for k, out in enumerate(outs):
            out[z] = back[k * size : (k + 1) * size]


def rows_stage(field, x_parts, parts_out):
    slab, bins, columns = field[0].shape
    length = x_parts[0].shape[1]
    block = min(8, slab)
    size = length // parts_out
    result = jax.ShapeDtypeStruct((slab, size, columns), jnp.bfloat16)
    macs = slab * 4 * length * length * columns
    return pl.pallas_call(
        functools.partial(rows_kernel, len(field)),
        grid=(slab // block,),
        in_specs=[
            *[pl.BlockSpec((block, bins, columns), lambda i: (i, 0, 0)) for _ in field],
            *[whole(t) for t in x_parts],
        ],
        out_specs=[pl.BlockSpec((block, size, columns), lambda i: (i, 0, 0))] * parts_out,
        out_shape=[result] * parts_out,
        compiler_params=PARAMS,
        cost_estimate=cost(4 * macs, [*field, *field]),
        name="rows",
    )(*field, *x_parts)


def image_kernel(pieces, *refs):
    field, (y_high, y_low), out = refs[:pieces], refs[pieces : pieces + 2], refs[-1]
    block, rows, columns = field[0].shape
    total = jnp.zeros((block * rows, out.shape[2]), jnp.float32)
    for part in range(pieces):
        piece = field[part][...].reshape(block * rows, columns)
        total = total + dot(piece, y_high[part]) + dot(piece, y_low[part])
    out[...] = total.reshape(out.shape)


def image_stage(field, y_parts, before, first, depth):
    slab, rows, columns = field[0].shape
    block = min(4, slab)
    skip = first // block
    width = y_parts[0].shape[2]
    result = jax.ShapeDtypeStruct((depth, rows, width), jnp.float32)
    held = [] if before is None else [before]
    macs = 2 * slab * rows * columns * len(field) * width
    return pl.pallas_call(
        functools.partial(image_kernel, len(field)),
        grid=(slab // block,),
        in_specs=[
            *[pl.BlockSpec((block, rows, columns), lambda i: (i, 0, 0)) for _ in field],
            *[whole(t) for t in y_parts],
            *[pl.BlockSpec(memory_space=pl.ANY) for _ in held],
        ],
        out_specs=pl.BlockSpec((block, rows, width), lambda i: (i + skip, 0, 0)),
        out_shape=result,
        input_output_aliases={len(field) + 2: 0} if held else {},
        compiler_params=PARAMS,
        cost_estimate=cost(4 * macs, [*field, *field]),
        name="image",
    )(*field, *y_parts, *held)


def from_offset(array, axis, size, offset):
    return lax.ppermute(array, axis, [(i, i ^ offset) for i in range(size)])


def on_device(slabs, parts, record, shifts, station_group, weights, psf_real, psf_imag):
    depth, bins, width = psf_real.shape
    stations = weights.shape[0]
    nx = weights.shape[1] * parts
    ny = weights.shape[2]
    gx, gy, sta = lax.axis_index("gx"), lax.axis_index("gy"), lax.axis_index("sta")
    count = lambda n: jnp.arange(n, dtype=jnp.int32)
    all_x, all_y, all_z = count(nx), count(ny), count(depth)
    own_b = gx * bins + count(bins)
    own_c = gy * width + count(width)
    order_x = [gx ^ k for k in range(slabs)]
    order_y = [gy ^ k for k in range(parts)]

    step = stations // 2
    gathered = [
        lax.all_gather(weights[k * step : (k + 1) * step], "gy", axis=0) for k in range(2)
    ]

    own = coefficients(record, shifts, station_counts(station_group), sta)
    coefficient = lax.all_gather(own, "gx", axis=0, tiled=True).astype(jnp.float32)
    cosine_z, sine_z = fourier_parts(all_z, all_z, depth, 1.0)
    coef_spectrum = jnp.dot(
        jnp.concatenate([cosine_z, -sine_z]), coefficient, precision=HIGHEST
    )
    coef_spectrum = jnp.where(sta == 0, coef_spectrum, jnp.roll(coef_spectrum, stations, axis=1))
    coef_high, coef_low = halves(coef_spectrum)
    coef = jnp.concatenate([coef_high, coef_low, coef_high[:, :stations]], axis=1)
    gathered[0], coef = lax.optimization_barrier((gathered[0], coef))

    cosine_y, sine_y = fourier_parts(all_y, own_c, ny, 1.0)
    cosine_x, sine_x = fourier_parts(own_b, all_x, nx, 1.0)
    y_forward = halves(jnp.concatenate([cosine_y, -sine_y], axis=1))
    x_forward = halves(jnp.concatenate([cosine_x, sine_x], axis=0))
    own_spectra = [lateral(g, y_forward, x_forward) for g in gathered]
    other = [from_offset(high, "sta", 2, 1) for high, _ in own_spectra]
    spectra = [*[high for high, _ in own_spectra], *other, *[low for _, low in own_spectra]]

    slab = depth // slabs
    size = slab // 2
    order_z = jnp.concatenate(
        [p * slab + h * size + count(size) for h in range(2) for p in order_x]
    )
    z_parts = halves(jnp.concatenate(fourier_parts(order_z, all_z, depth, 1.0 / depth)))
    splits = 2 if bins // 2 % BLOCK == 0 else 1
    width_b = bins // splits
    fields = [
        depth_stage(
            coef, spectra, psf_real, psf_imag, z_parts, 2 * slabs, k * width_b, width_b
        )
        for k in range(splits)
    ]

    order_b = jnp.concatenate(
        [p * bins + k * width_b + count(width_b) for k in range(splits) for p in order_x]
    )
    x_rows = jnp.concatenate([p * (nx // parts) + count(nx // parts) for p in order_y])
    x_parts = halves(jnp.concatenate(fourier_parts(x_rows, order_b, nx, 1.0 / nx)))
    cosine_back, sine_back = zip(
        *[fourier_parts(p * width + count(width), all_y, ny, 1.0 / ny) for p in order_y]
    )
    y_parts = halves(
        jnp.stack([jnp.concatenate([c, -s]) for c, s in zip(cosine_back, sine_back)])
    )

    image = None
    arrived = None
    rows = None
    for h in range(2):
        pieces = []
        for k in range(splits):
            sent = list(fields[k][h * slabs : (h + 1) * slabs])
            if arrived is not None:
                if rows is not None and k == splits - 1:
                    sent, arrived, rows = lax.optimization_barrier((sent, arrived, rows))
                else:
                    sent, arrived = lax.optimization_barrier((sent, arrived))
            landed = [sent[0]] + [
                from_offset(sent[p], "gx", slabs, p) for p in range(1, slabs)
            ]
            arrived = landed[1:]
            pieces += landed
        rows = rows_stage(pieces, x_parts, parts)
        ready = [rows[0]] + [from_offset(rows[p], "gy", parts, p) for p in range(1, parts)]
        image = image_stage(ready, y_parts, image, h * size, slab)
    return image[None]


def solution(mesh):
    in_specs = (
        P(),
        P(None, "gx"),
        P(),
        P("sta", "gy", None),
        P(None, "gx", "gy"),
        P(None, "gx", "gy"),
    )
    out_specs = P("sta", "gx", "gy", None)
    return jax.shard_map(
        functools.partial(on_device, mesh.shape["gx"], mesh.shape["gy"]),
        mesh=mesh,
        in_specs=in_specs,
        out_specs=out_specs,
        check_vma=False,
    )
```

time: 1800 us -> 516 us (0.29)
  waiting for transfers between devices: 759 us -> 275 us
  blocking collectives: 374 us -> 14.9 us
  local copies, waits for them, and re-layouts: 344 us -> 11.1 us
  matrix products: 194 us -> 0.51 us
  Pallas kernels: 0 us -> 132 us
  other arithmetic: 89.5 us -> 20.6 us
  starting transfers between devices: 21.3 us -> 42.7 us
    all_to_all x3 -> x0, waiting for transfers between devices: 721 us -> none  [the longest x1 361 us: on_device(): lax.all_to_all(by_rows, 'gx', split_axis=3, concat_axis=2, tiled=True)]
    all_to_all x1 -> x0, blocking collectives: 374 us -> none  [on_device(): lax.all_to_all(back_depth, 'gx', split_axis=2, concat_axis=3, tiled=True)]
    dot_general x7 -> x1, matrix products: 194 us -> 0.37 us  [on_device(): jnp.dot(jnp.concatenate([cosine_z, -sine_z]), coefficient, precision=HIGH...]
    ppermute x0 -> x20, waiting for transfers between devices: none -> 178 us  [from_offset(): return lax.ppermute(array, axis, [(i, i ^ offset) for i in range(size)])]
    pallas_call x0 -> x8, Pallas kernels: none -> 132 us  [the longest x2 60.5 us: depth_stage(): pl.pallas_call(functools.partial(depth_kernel, len(spectra), outs), grid=...]
    unnamed x9 -> x42, local copies, waits for them, and re-layouts: 98.3 us -> 5.98 us
    transpose x4 -> x0, local copies, waits for them, and re-layouts: 88.3 us -> none  [the longest x2 37.7 us: along_rows(): return jnp.einsum('itzny,oikn->otzky', piece, table, precision=HIGHEST)]
    gather x3 -> x0, local copies, waits for them, and re-layouts: 65.1 us -> none  [coefficients(): jnp.take_along_axis(record, positions.reshape(positions.shape[0], -1), ax...]
  transfers between devices with their start and end apart: 4 -> 22, of which waited for: 4 -> 14; matrix products, arithmetic and copies ran while one was open for 4% -> 4% of each run, Pallas kernels for 0% -> 10%
where the time goes in v1:
time: 516 us; the launch traced here: 511 us
  waiting for transfers between devices  275 us (53%)
  Pallas kernels  132 us (26%)
  starting transfers between devices  42.7 us (8%)
  other arithmetic  20.6 us (4%)
  blocking collectives  14.9 us (3%)
  between operations  14 us (3%)
  local copies, waits for them, and re-layouts  11.1 us (2%)
    ppermute x20, waiting for transfers between devices, from_offset(): return lax.ppermute(array, axis, [(i, i ^ offset) for i in range(size)])  178 us
    all_gather x2, waiting for transfers between devices, on_device(): lax.all_gather(weights[k * step:(k + 1) * step], 'gy', axis=0)  96.1 us
    pallas_call x2, Pallas kernels, depth_stage(): pl.pallas_call(functools.partial(depth_kernel, len(spectra), outs), grid=...  60.5 us
    ppermute x20, starting transfers between devices, from_offset(): return lax.ppermute(array, axis, [(i, i ^ offset) for i in range(size)])  42.7 us
    pallas_call x2, Pallas kernels, lateral(): pl.pallas_call(lateral_kernel, grid=(stations // BLOCK,), in_specs=[pl.Bl...  39.2 us
    pallas_call x2, Pallas kernels, image_stage(): pl.pallas_call(functools.partial(image_kernel, len(field)), grid=(slab //...  18.6 us
    all_gather x1, blocking collectives, on_device(): lax.all_gather(own, 'gx', axis=0, tiled=True).astype(jnp.float32)  14.9 us
    pallas_call x2, Pallas kernels, rows_stage(): pl.pallas_call(functools.partial(rows_kernel, len(field)), grid=(slab //...  14.1 us
  transfers between devices with their start and end apart: 22, of which 14 were waited for; matrix products, arithmetic and copies ran while one was open for 4% of the time, Pallas kernels for 10%

profile of v1, /device:TPU:0, one launch (start us, length us, event | category | flops | bytes accessed | tf_op | source)
XLA Modules:
  0.0 511.1 jit_solution(3310992973702369504)
XLA Ops:
  18.1 14.9 %all_gather.17 = bf16[256,128]{1,0:T(8,128)(2,1)S(1)} all-gather(bf16[64,128]{1,0:T(8,128)(2,1)S(1)} %copy.17), channel_id=1, replica_groups=mesh['sta'=2,'gx'=4,'gy'=4] {'gx'}, dimensions={0}, use_global_device_ids=true | all-gather | bytes 81920 | tf_op jit(solution)/shard_map/all_gather | solution.py:270
  36.3 36.2 %all-gather.5.cloned.1.call-done = bf16[128,64,512]{2,1,0:T(8,128)(2,1)} async-done(((bf16[32,64,512]{2,1,0:T(8,128)(2,1)}), bf16[128,64,512]{2,1,0:T(8,128)(2,1)}) %all-gather.5.cloned.1.call-update) | async-done | bytes 8388624 | tf_op jit(solution)/shard_map/all_gather | solution.py:266
  72.5 59.9 %all-gather.7.cloned.1.call-done = bf16[128,64,512]{2,1,0:T(8,128)(2,1)} async-done(((bf16[32,64,512]{2,1,0:T(8,128)(2,1)}), bf16[128,64,512]{2,1,0:T(8,128)(2,1)}) %all-gather.7.cloned.1.call-update) | async-done | bytes 8388624 | tf_op jit(solution)/shard_map/all_gather | solution.py:266
  132.4 19.3 %lateral.3 = (bf16[64,32,256]{2,1,0:T(8,128)(2,1)S(1)}, bf16[64,32,256]{2,1,0:T(8,128)(2,1)S(1)}) custom-call(bf16[4,32,64,512]{3,2,1,0:T(8,128)(2,1)} %bitcast.22, bf16[512,256]{1,0:T(8,128)(2,1)S(1)} %get-tuple-element.100.y_high, bf16[512,256]{1,0:T(8,128)(2,1)S(1)} %get-tuple-element.99.y_low, bf16[128,256]{1,0:T(8,128)(2,1)S(1)} %get-tuple-element.104.x_high, ...), custom_call_target="tpu_custom_call" | custom-call | flops 11811160064 | bytes 10485760 | tf_op jit(solution)/shard_map/lateral/pallas_call | solution.py:95
  151.7 19.9 %lateral.2 = (bf16[64,32,256]{2,1,0:T(8,128)(2,1)S(1)}, bf16[64,32,256]{2,1,0:T(8,128)(2,1)S(1)}) custom-call(bf16[4,32,64,512]{3,2,1,0:T(8,128)(2,1)} %bitcast.21, bf16[512,256]{1,0:T(8,128)(2,1)S(1)} %get-tuple-element.100.y_high, bf16[512,256]{1,0:T(8,128)(2,1)S(1)} %get-tuple-element.99.y_low, bf16[128,256]{1,0:T(8,128)(2,1)S(1)} %get-tuple-element.104.x_high, ...), custom_call_target="tpu_custom_call" | custom-call | flops 11811160064 | bytes 10485760 | tf_op jit(solution)/shard_map/lateral/pallas_call | solution.py:95
  177.2 21.6 %collective-permute-done.refs_2_ = bf16[64,32,256]{2,1,0:T(8,128)(2,1)} collective-permute-done((bf16[64,32,256]{2,1,0:T(8,128)(2,1)S(1)}, bf16[64,32,256]{2,1,0:T(8,128)(2,1)}, u32[]{:S(2)}, u32[]{:S(2)}) %collective-permute-start) | collective-permute-done | bytes 1048608 | tf_op jit(solution)/shard_map/ppermute | solution.py:248
  198.7 21.8 %collective-permute-done.1.refs_3_ = bf16[64,32,256]{2,1,0:T(8,128)(2,1)} collective-permute-done((bf16[64,32,256]{2,1,0:T(8,128)(2,1)S(1)}, bf16[64,32,256]{2,1,0:T(8,128)(2,1)}, u32[]{:S(2)}, u32[]{:S(2)}) %collective-permute-start.1) | collective-permute-done | bytes 1048608 | tf_op jit(solution)/shard_map/ppermute | solution.py:248
  220.5 30.2 %depth.2 = (bf16[32,32,256]{2,1,0:T(8,128)(2,1)S(1)}, bf16[32,32,256]{2,1,0:T(8,128)(2,1)S(1)}, bf16[32,32,256]{2,1,0:T(8,128)(2,1)S(1)}, bf16[32,32,256]{2,1,0:...) custom-call(bf16[512,320]{1,0:T(8,128)(2,1)S(1)} %pad_maximum_fusion, ...), custom_call_target="tpu_custom_call" | custom-call | flops 18253611008 | bytes 16777216 | tf_op jit(solution)/shard_map/depth/pallas_call | solution.py:151
  256.0 30.2 %depth.3 = (bf16[32,32,256]{2,1,0:T(8,128)(2,1)S(1)}, bf16[32,32,256]{2,1,0:T(8,128)(2,1)S(1)}, bf16[32,32,256]{2,1,0:T(8,128)(2,1)S(1)}, bf16[32,32,256]{2,1,0:...) custom-call(bf16[512,320]{1,0:T(8,128)(2,1)S(1)} %pad_maximum_fusion, ...), custom_call_target="tpu_custom_call" | custom-call | flops 18253611008 | bytes 16777216 | tf_op jit(solution)/shard_map/depth/pallas_call | solution.py:151
  291.3 10.0 %collective-permute-start.5 = (bf16[32,32,256]{2,1,0:T(8,128)(2,1)S(1)}, bf16[32,32,256]{2,1,0:T(8,128)(2,1)S(1)}, u32[]{:S(2)}, u32[]{:S(2)}) collective-permute-start(bf16[32,32,256]{2,1,0:T(8,128)(2,1)S(1)} %get-tuple-element.64), channel_id=1, source_target_pairs={{0,4},{4,0},{8,12},{12,8},{1,5},{5,1},{9,13},{13,9},{2,6},{6,2},{1... | collective-permute-start | bytes 1572872 | tf_op jit(solution)/shard_map/ppermute | solution.py:248
  307.5 13.8 %collective-permute-done.5.refs_5_ = bf16[32,32,256]{2,1,0:T(8,128)(2,1)S(1)} collective-permute-done((bf16[32,32,256]{2,1,0:T(8,128)(2,1)S(1)}, bf16[32,32,256]{2,1,0:T(8,128)(2,1)S(1)}, u32[]{:S(2)}, u32[]{:S(2)}) %collective-permute-start.5) | collective-permute-done | bytes 524320 | tf_op jit(solution)/shard_map/ppermute | solution.py:248
  321.3 18.2 %collective-permute-done.6.refs_6_ = bf16[32,32,256]{2,1,0:T(8,128)(2,1)S(1)} collective-permute-done((bf16[32,32,256]{2,1,0:T(8,128)(2,1)S(1)}, bf16[32,32,256]{2,1,0:T(8,128)(2,1)S(1)}, u32[]{:S(2)}, u32[]{:S(2)}) %collective-permute-start.6) | collective-permute-done | bytes 524320 | tf_op jit(solution)/shard_map/ppermute | solution.py:248
  339.5 8.8 %collective-permute-start.8 = (bf16[32,32,256]{2,1,0:T(8,128)(2,1)S(1)}, bf16[32,32,256]{2,1,0:T(8,128)(2,1)S(1)}, u32[]{:S(2)}, u32[]{:S(2)}) collective-permute-start(bf16[32,32,256]{2,1,0:T(8,128)(2,1)S(1)} %get-tuple-element.68), channel_id=1, source_target_pairs={{0,4},{4,0},{8,12},{12,8},{1,5},{5,1},{9,13},{13,9},{2,6},{6,2},{1... | collective-permute-start | bytes 1572872 | tf_op jit(solution)/shard_map/ppermute | solution.py:248
  350.8 7.0 %rows.2 = (bf16[32,64,256]{2,1,0:T(8,128)(2,1)}, bf16[32,64,256]{2,1,0:T(8,128)(2,1)}, bf16[32,64,256]{2,1,0:T(8,128)(2,1)}, bf16[32,64,256]{2,1,0:T(8,128)(2,1)}) custom-call(bf16[32,32,256]{2,1,0:T(8,128)(2,1)S(1)} %get-tuple-element.75.refs_0_, bf16[32,32,256]{2,1,0:T(8,128)(2,1)S(1)} %collective-permute-done.2.refs_1_, ...), custom_call_target="tpu_custom_call" | custom-call | flops 8589934592 | bytes 8388608 | tf_op jit(solution)/shard_map/rows/pallas_call | solution.py:197
  357.8 8.8 %collective-permute-done.8.refs_1_ = bf16[32,32,256]{2,1,0:T(8,128)(2,1)S(1)} collective-permute-done((bf16[32,32,256]{2,1,0:T(8,128)(2,1)S(1)}, bf16[32,32,256]{2,1,0:T(8,128)(2,1)S(1)}, u32[]{:S(2)}, u32[]{:S(2)}) %collective-permute-start.8) | collective-permute-done | bytes 524320 | tf_op jit(solution)/shard_map/ppermute | solution.py:248
  366.6 20.0 %collective-permute-done.9.refs_2_ = bf16[32,32,256]{2,1,0:T(8,128)(2,1)S(1)} collective-permute-done((bf16[32,32,256]{2,1,0:T(8,128)(2,1)S(1)}, bf16[32,32,256]{2,1,0:T(8,128)(2,1)S(1)}, u32[]{:S(2)}, u32[]{:S(2)}) %collective-permute-start.9) | collective-permute-done | bytes 524320 | tf_op jit(solution)/shard_map/ppermute | solution.py:248
  386.6 7.7 %collective-permute-start.11 = (bf16[32,32,256]{2,1,0:T(8,128)(2,1)S(1)}, bf16[32,32,256]{2,1,0:T(8,128)(2,1)S(1)}, u32[]{:S(2)}, u32[]{:S(2)}) collective-permute-start(bf16[32,32,256]{2,1,0:T(8,128)(2,1)S(1)} %get-tuple-element.82), channel_id=1, source_target_pairs={{0,4},{4,0},{8,12},{12,8},{1,5},{5,1},{9,13},{13,9},{2,6},{6,2},{1... | collective-permute-start | bytes 1572872 | tf_op jit(solution)/shard_map/ppermute | solution.py:248
  401.6 9.1 %collective-permute-done.11.refs_5_ = bf16[32,32,256]{2,1,0:T(8,128)(2,1)S(1)} collective-permute-done((bf16[32,32,256]{2,1,0:T(8,128)(2,1)S(1)}, bf16[32,32,256]{2,1,0:T(8,128)(2,1)S(1)}, u32[]{:S(2)}, u32[]{:S(2)}) %collective-permute-start.11) | collective-permute-done | bytes 524320 | tf_op jit(solution)/shard_map/ppermute | solution.py:248
  410.7 22.1 %collective-permute-done.12.refs_6_ = bf16[32,32,256]{2,1,0:T(8,128)(2,1)} collective-permute-done((bf16[32,32,256]{2,1,0:T(8,128)(2,1)}, bf16[32,32,256]{2,1,0:T(8,128)(2,1)}, u32[]{:S(2)}, u32[]{:S(2)}) %collective-permute-start.12) | collective-permute-done | bytes 524320 | tf_op jit(solution)/shard_map/ppermute | solution.py:248
  434.9 7.1 %rows.3 = (bf16[32,64,256]{2,1,0:T(8,128)(2,1)}, bf16[32,64,256]{2,1,0:T(8,128)(2,1)}, bf16[32,64,256]{2,1,0:T(8,128)(2,1)}, bf16[32,64,256]{2,1,0:T(8,128)(2,1)}) custom-call(bf16[32,32,256]{2,1,0:T(8,128)(2,1)S(1)} %copy-done.7, bf16[32,32,256]{2,1,0:T(8,128)(2,1)S(1)} %collective-permute-done.8.refs_1_, ...), custom_call_target="tpu_custom_call" | custom-call | flops 8589934592 | bytes 8388608 | tf_op jit(solution)/shard_map/rows/pallas_call | solution.py:197
  449.8 9.3 %image.2.refs_6_ = f32[64,64,512]{2,1,0:T(8,128)} custom-call(bf16[32,64,256]{2,1,0:T(8,128)(2,1)S(1)} %copy-done.3, bf16[32,64,256]{2,1,0:T(8,128)(2,1)S(1)} %collective-permute-done.17.refs_1_, bf16[32,64,256]{2,1,0:T(8,128)(2,1)S(1)} %collective-permute-done.18.refs_2_, bf16[32,64,256]{2,1,0:T(8,128)(2,1)} %copy-done.14, ...), custom_call_target="tpu_custom_call" | custom-call | flops 8589934592 | bytes 8388608 | tf_op jit(solution)/shard_map/image/pallas_call | solution.py:230
  459.2 13.0 %collective-permute-done.15.refs_2_ = bf16[32,64,256]{2,1,0:T(8,128)(2,1)S(1)} collective-permute-done((bf16[32,64,256]{2,1,0:T(8,128)(2,1)}, bf16[32,64,256]{2,1,0:T(8,128)(2,1)S(1)}, u32[]{:S(2)}, u32[]{:S(2)}) %collective-permute-start.15) | collective-permute-done | bytes 1048608 | tf_op jit(solution)/shard_map/ppermute | solution.py:248
  472.1 21.6 %collective-permute-done.16.refs_3_ = bf16[32,64,256]{2,1,0:T(8,128)(2,1)S(1)} collective-permute-done((bf16[32,64,256]{2,1,0:T(8,128)(2,1)}, bf16[32,64,256]{2,1,0:T(8,128)(2,1)S(1)}, u32[]{:S(2)}, u32[]{:S(2)}) %collective-permute-start.16) | collective-permute-done | bytes 1048608 | tf_op jit(solution)/shard_map/ppermute | solution.py:248
  494.8 9.2 %image.3 = f32[64,64,512]{2,1,0:T(8,128)} custom-call(bf16[32,64,256]{2,1,0:T(8,128)(2,1)S(1)} %copy-done.2, bf16[32,64,256]{2,1,0:T(8,128)(2,1)S(1)} %collective-permute-done.14.refs_1_, bf16[32,64,256]{2,1,0:T(8,128)(2,1)S(1)} %collective-permute-done.15.refs_2_, bf16[32,64,256]{2,1,0:T(8,128)(2,1)} %copy-done.15, ...), custom_call_target="tpu_custom_call", output_to_operand_aliasing={{}: (6, {})} | custom-call | flops 8589934592 | bytes 8388608 | tf_op jit(solution)/shard_map/image/pallas_call | solution.py:230
  (114 shorter events, 57.4 us)
Async XLA Ops:
  6.5 65.9 %all-gather.5.cloned.1.call-start = ((), (), s32[]{:S(2)}) async-start(), calls=%async_computation | async-start | bytes 10485760 | tf_op jit(solution)/shard_map/all_gather | solution.py:266
  11.3 121.1 %all-gather.7.cloned.1.call-start = ((), (), s32[]{:S(2)}) async-start(), calls=%async_computation.1 | async-start | bytes 10485760 | tf_op jit(solution)/shard_map/all_gather | solution.py:266
  172.6 26.1 %collective-permute-start = (bf16[64,32,256]{2,1,0:T(8,128)(2,1)S(1)}, bf16[64,32,256]{2,1,0:T(8,128)(2,1)}, u32[]{:S(2)}, u32[]{:S(2)}) collective-permute-start(bf16[64,32,256]{2,1,0:T(8,128)(2,1)S(1)} %get-tuple-element.49.refs_0_), channel_id=1, source_target_pairs={{0,16},{16,0},{1,17},{17,1},{2,18},{18,2},{3,19},{19,3},{4,20},{20... | collective-permute-start | bytes 3145736 | tf_op jit(solution)/shard_map/ppermute | solution.py:248
  174.1 46.4 %collective-permute-start.1 = (bf16[64,32,256]{2,1,0:T(8,128)(2,1)S(1)}, bf16[64,32,256]{2,1,0:T(8,128)(2,1)}, u32[]{:S(2)}, u32[]{:S(2)}) collective-permute-start(bf16[64,32,256]{2,1,0:T(8,128)(2,1)S(1)} %get-tuple-element.50.refs_1_), channel_id=1, source_target_pairs={{0,16},{16,0},{1,17},{17,1},{2,18},{18,2},{3,19},{19,3},{4,20},{20... | collective-permute-start | bytes 3145736 | tf_op jit(solution)/shard_map/ppermute | solution.py:248
  251.6 34.6 %collective-permute-start.2 = (bf16[32,32,256]{2,1,0:T(8,128)(2,1)S(1)}, bf16[32,32,256]{2,1,0:T(8,128)(2,1)S(1)}, u32[]{:S(2)}, u32[]{:S(2)}) collective-permute-start(bf16[32,32,256]{2,1,0:T(8,128)(2,1)S(1)} %get-tuple-element.61), channel_id=1, source_target_pairs={{0,4},{4,0},{8,12},{12,8},{1,5},{5,1},{9,13},{13,9},{2,6},{6,2},{1... | collective-permute-start | bytes 1572872 | tf_op jit(solution)/shard_map/ppermute | solution.py:248
  253.1 38.2 %collective-permute-start.3 = (bf16[32,32,256]{2,1,0:T(8,128)(2,1)S(1)}, bf16[32,32,256]{2,1,0:T(8,128)(2,1)S(1)}, u32[]{:S(2)}, u32[]{:S(2)}) collective-permute-start(bf16[32,32,256]{2,1,0:T(8,128)(2,1)S(1)} %get-tuple-element.62), channel_id=1, source_target_pairs={{0,8},{4,12},{8,0},{12,4},{1,9},{5,13},{9,1},{13,5},{2,10},{6,14},... | collective-permute-start | bytes 1572872 | tf_op jit(solution)/shard_map/ppermute | solution.py:248
  255.5 92.9 %copy-start.17 = (bf16[32,32,256]{2,1,0:T(8,128)(2,1)S(1)}, bf16[32,32,256]{2,1,0:T(8,128)(2,1)}, u32[]{:S(2)}) copy-start(bf16[32,32,256]{2,1,0:T(8,128)(2,1)} %get-tuple-element.69) | copy-start | bytes 1572868
  255.5 93.8 %copy-start.16 = (bf16[32,32,256]{2,1,0:T(8,128)(2,1)S(1)}, bf16[32,32,256]{2,1,0:T(8,128)(2,1)}, u32[]{:S(2)}) copy-start(bf16[32,32,256]{2,1,0:T(8,128)(2,1)} %get-tuple-element.70) | copy-start | bytes 1572868
  255.5 35.8 %collective-permute-start.4 = (bf16[32,32,256]{2,1,0:T(8,128)(2,1)S(1)}, bf16[32,32,256]{2,1,0:T(8,128)(2,1)S(1)}, u32[]{:S(2)}, u32[]{:S(2)}) collective-permute-start(bf16[32,32,256]{2,1,0:T(8,128)(2,1)S(1)} %get-tuple-element.63), channel_id=1, source_target_pairs={{0,12},{4,8},{8,4},{12,0},{1,13},{5,9},{9,5},{13,1},{2,14},{6,10},... | collective-permute-start | bytes 1572872 | tf_op jit(solution)/shard_map/ppermute | solution.py:248
  291.3 30.0 %collective-permute-start.5 = (bf16[32,32,256]{2,1,0:T(8,128)(2,1)S(1)}, bf16[32,32,256]{2,1,0:T(8,128)(2,1)S(1)}, u32[]{:S(2)}, u32[]{:S(2)}) collective-permute-start(bf16[32,32,256]{2,1,0:T(8,128)(2,1)S(1)} %get-tuple-element.64), channel_id=1, source_target_pairs={{0,4},{4,0},{8,12},{12,8},{1,5},{5,1},{9,13},{13,9},{2,6},{6,2},{1... | collective-permute-start | bytes 1572872 | tf_op jit(solution)/shard_map/ppermute | solution.py:248
  301.3 38.2 %collective-permute-start.6 = (bf16[32,32,256]{2,1,0:T(8,128)(2,1)S(1)}, bf16[32,32,256]{2,1,0:T(8,128)(2,1)S(1)}, u32[]{:S(2)}, u32[]{:S(2)}) collective-permute-start(bf16[32,32,256]{2,1,0:T(8,128)(2,1)S(1)} %get-tuple-element.65), channel_id=1, source_target_pairs={{0,8},{4,12},{8,0},{12,4},{1,9},{5,13},{9,1},{13,5},{2,10},{6,14},... | collective-permute-start | bytes 1572872 | tf_op jit(solution)/shard_map/ppermute | solution.py:248
  302.2 37.3 %collective-permute-start.7 = (bf16[32,32,256]{2,1,0:T(8,128)(2,1)S(1)}, bf16[32,32,256]{2,1,0:T(8,128)(2,1)S(1)}, u32[]{:S(2)}, u32[]{:S(2)}) collective-permute-start(bf16[32,32,256]{2,1,0:T(8,128)(2,1)S(1)} %get-tuple-element.66), channel_id=1, source_target_pairs={{0,12},{4,8},{8,4},{12,0},{1,13},{5,9},{9,5},{13,1},{2,14},{6,10},... | collective-permute-start | bytes 1572872 | tf_op jit(solution)/shard_map/ppermute | solution.py:248
  339.5 27.1 %collective-permute-start.8 = (bf16[32,32,256]{2,1,0:T(8,128)(2,1)S(1)}, bf16[32,32,256]{2,1,0:T(8,128)(2,1)S(1)}, u32[]{:S(2)}, u32[]{:S(2)}) collective-permute-start(bf16[32,32,256]{2,1,0:T(8,128)(2,1)S(1)} %get-tuple-element.68), channel_id=1, source_target_pairs={{0,4},{4,0},{8,12},{12,8},{1,5},{5,1},{9,13},{13,9},{2,6},{6,2},{1... | collective-permute-start | bytes 1572872 | tf_op jit(solution)/shard_map/ppermute | solution.py:248
  348.3 38.2 %collective-permute-start.9 = (bf16[32,32,256]{2,1,0:T(8,128)(2,1)S(1)}, bf16[32,32,256]{2,1,0:T(8,128)(2,1)S(1)}, u32[]{:S(2)}, u32[]{:S(2)}) collective-permute-start(bf16[32,32,256]{2,1,0:T(8,128)(2,1)S(1)} %copy-done.17), channel_id=1, source_target_pairs={{0,8},{4,12},{8,0},{12,4},{1,9},{5,13},{9,1},{13,5},{2,10},{6,14},... | collective-permute-start | bytes 1572872 | tf_op jit(solution)/shard_map/ppermute | solution.py:248
  349.3 37.2 %collective-permute-start.10 = (bf16[32,32,256]{2,1,0:T(8,128)(2,1)S(1)}, bf16[32,32,256]{2,1,0:T(8,128)(2,1)S(1)}, u32[]{:S(2)}, u32[]{:S(2)}) collective-permute-start(bf16[32,32,256]{2,1,0:T(8,128)(2,1)S(1)} %copy-done.16), channel_id=1, source_target_pairs={{0,12},{4,8},{8,4},{12,0},{1,13},{5,9},{9,5},{13,1},{2,14},{6,10},... | collective-permute-start | bytes 1572872 | tf_op jit(solution)/shard_map/ppermute | solution.py:248
  386.6 24.1 %collective-permute-start.11 = (bf16[32,32,256]{2,1,0:T(8,128)(2,1)S(1)}, bf16[32,32,256]{2,1,0:T(8,128)(2,1)S(1)}, u32[]{:S(2)}, u32[]{:S(2)}) collective-permute-start(bf16[32,32,256]{2,1,0:T(8,128)(2,1)S(1)} %get-tuple-element.82), channel_id=1, source_target_pairs={{0,4},{4,0},{8,12},{12,8},{1,5},{5,1},{9,13},{13,9},{2,6},{6,2},{1... | collective-permute-start | bytes 1572872 | tf_op jit(solution)/shard_map/ppermute | solution.py:248
  394.2 38.5 %collective-permute-start.12 = (bf16[32,32,256]{2,1,0:T(8,128)(2,1)}, bf16[32,32,256]{2,1,0:T(8,128)(2,1)}, u32[]{:S(2)}, u32[]{:S(2)}) collective-permute-start(bf16[32,32,256]{2,1,0:T(8,128)(2,1)} %get-tuple-element.83), channel_id=1, source_target_pairs={{0,8},{4,12},{8,0},{12,4},{1,9},{5,13},{9,1},{13,5},{2,10},{6,14},... | collective-permute-start | bytes 1572872 | tf_op jit(solution)/shard_map/ppermute | solution.py:248
  395.2 37.6 %collective-permute-start.13 = (bf16[32,32,256]{2,1,0:T(8,128)(2,1)}, bf16[32,32,256]{2,1,0:T(8,128)(2,1)}, u32[]{:S(2)}, u32[]{:S(2)}) collective-permute-start(bf16[32,32,256]{2,1,0:T(8,128)(2,1)} %get-tuple-element.84), channel_id=1, source_target_pairs={{0,12},{4,8},{8,4},{12,0},{1,13},{5,9},{9,5},{13,1},{2,14},{6,10},... | collective-permute-start | bytes 1572872 | tf_op jit(solution)/shard_map/ppermute | solution.py:248
  399.7 42.9 %collective-permute-start.17 = (bf16[32,64,256]{2,1,0:T(8,128)(2,1)}, bf16[32,64,256]{2,1,0:T(8,128)(2,1)S(1)}, u32[]{:S(2)}, u32[]{:S(2)}) collective-permute-start(bf16[32,64,256]{2,1,0:T(8,128)(2,1)} %get-tuple-element.78), channel_id=1, source_target_pairs={{0,1},{1,0},{2,3},{3,2},{4,5},{5,4},{6,7},{7,6},{8,9},{9,8},{10,11... | collective-permute-start | bytes 3145736 | tf_op jit(solution)/shard_map/ppermute | solution.py:248
  400.9 44.7 %collective-permute-start.18 = (bf16[32,64,256]{2,1,0:T(8,128)(2,1)}, bf16[32,64,256]{2,1,0:T(8,128)(2,1)S(1)}, u32[]{:S(2)}, u32[]{:S(2)}) collective-permute-start(bf16[32,64,256]{2,1,0:T(8,128)(2,1)} %get-tuple-element.79), channel_id=1, source_target_pairs={{0,2},{1,3},{2,0},{3,1},{4,6},{5,7},{6,4},{7,5},{8,10},{9,11},{10,... | collective-permute-start | bytes 3145736 | tf_op jit(solution)/shard_map/ppermute | solution.py:248
  410.7 38.1 %collective-permute-start.19 = (bf16[32,64,256]{2,1,0:T(8,128)(2,1)}, bf16[32,64,256]{2,1,0:T(8,128)(2,1)S(1)}, u32[]{:S(2)}, u32[]{:S(2)}) collective-permute-start(bf16[32,64,256]{2,1,0:T(8,128)(2,1)} %get-tuple-element.80), channel_id=1, source_target_pairs={{0,3},{1,2},{2,1},{3,0},{4,7},{5,6},{6,5},{7,4},{8,11},{9,10},{10,... | collective-permute-start | bytes 3145736 | tf_op jit(solution)/shard_map/ppermute | solution.py:248
  441.9 17.2 %collective-permute-start.14 = (bf16[32,64,256]{2,1,0:T(8,128)(2,1)}, bf16[32,64,256]{2,1,0:T(8,128)(2,1)S(1)}, u32[]{:S(2)}, u32[]{:S(2)}) collective-permute-start(bf16[32,64,256]{2,1,0:T(8,128)(2,1)} %get-tuple-element.86), channel_id=1, source_target_pairs={{0,1},{1,0},{2,3},{3,2},{4,5},{5,4},{6,7},{7,6},{8,9},{9,8},{10,11... | collective-permute-start | bytes 3145736 | tf_op jit(solution)/shard_map/ppermute | solution.py:248
  441.9 30.2 %collective-permute-start.15 = (bf16[32,64,256]{2,1,0:T(8,128)(2,1)}, bf16[32,64,256]{2,1,0:T(8,128)(2,1)S(1)}, u32[]{:S(2)}, u32[]{:S(2)}) collective-permute-start(bf16[32,64,256]{2,1,0:T(8,128)(2,1)} %get-tuple-element.87), channel_id=1, source_target_pairs={{0,2},{1,3},{2,0},{3,1},{4,6},{5,7},{6,4},{7,5},{8,10},{9,11},{10,... | collective-permute-start | bytes 3145736 | tf_op jit(solution)/shard_map/ppermute | solution.py:248
  442.6 51.2 %collective-permute-start.16 = (bf16[32,64,256]{2,1,0:T(8,128)(2,1)}, bf16[32,64,256]{2,1,0:T(8,128)(2,1)S(1)}, u32[]{:S(2)}, u32[]{:S(2)}) collective-permute-start(bf16[32,64,256]{2,1,0:T(8,128)(2,1)} %get-tuple-element.88), channel_id=1, source_target_pairs={{0,3},{1,2},{2,1},{3,0},{4,7},{5,6},{6,5},{7,4},{8,11},{9,10},{10,... | collective-permute-start | bytes 3145736 | tf_op jit(solution)/shard_map/ppermute | solution.py:248
  (19 other events, 334.1 us)
Sparse Core Ops, SparseCore 0:
  11.4 60.9 all-gather.4
  74.0 58.3 all-gather.6

commit v2 on v1

--- a/solution.py
+++ b/solution.py
@@ -281,7 +281,9 @@
     cosine_x, sine_x = fourier_parts(own_b, all_x, nx, 1.0)
     y_forward = halves(jnp.concatenate([cosine_y, -sine_y], axis=1))
     x_forward = halves(jnp.concatenate([cosine_x, sine_x], axis=0))
-    own_spectra = [lateral(g, y_forward, x_forward) for g in gathered]
+    own_spectra = [lateral(gathered[0], y_forward, x_forward)]
+    gathered[1], own_spectra[0] = lax.optimization_barrier((gathered[1], own_spectra[0]))
+    own_spectra.append(lateral(gathered[1], y_forward, x_forward))
     other = [from_offset(high, "sta", 2, 1) for high, _ in own_spectra]
     spectra = [*[high for high, _ in own_spectra], *other, *[low for _, low in own_spectra]]
 

time: 516 us -> 496 us (0.961)
  waiting for transfers between devices: 275 us -> 255 us
    all_gather x2, waiting for transfers between devices: 96.1 us -> 75.8 us  [on_device(): lax.all_gather(weights[k * step:(k + 1) * step], 'gy', axis=0)]
  transfers between devices with their start and end apart: 22 -> 22, of which waited for: 14 -> 14; matrix products, arithmetic and copies ran while one was open for 4% -> 4% of each run, Pallas kernels for 10% -> 15%
where the time goes in v2:
time: 496 us; the launch traced here: 491 us
  waiting for transfers between devices  255 us (51%)
  Pallas kernels  132 us (27%)
  starting transfers between devices  42.8 us (9%)
  other arithmetic  20.6 us (4%)
  blocking collectives  14.9 us (3%)
  between operations  14 us (3%)
  local copies, waits for them, and re-layouts  12.1 us (2%)
    ppermute x20, waiting for transfers between devices, from_offset(): return lax.ppermute(array, axis, [(i, i ^ offset) for i in range(size)])  178 us
    all_gather x2, waiting for transfers between devices, on_device(): lax.all_gather(weights[k * step:(k + 1) * step], 'gy', axis=0)  75.8 us
    pallas_call x2, Pallas kernels, depth_stage(): pl.pallas_call(functools.partial(depth_kernel, len(spectra), outs), grid=...  60.5 us
    ppermute x20, starting transfers between devices, from_offset(): return lax.ppermute(array, axis, [(i, i ^ offset) for i in range(size)])  42.7 us
    pallas_call x2, Pallas kernels, lateral(): pl.pallas_call(lateral_kernel, grid=(stations // BLOCK,), in_specs=[pl.Bl...  38.4 us
    pallas_call x2, Pallas kernels, image_stage(): pl.pallas_call(functools.partial(image_kernel, len(field)), grid=(slab //...  18.6 us
    all_gather x1, blocking collectives, on_device(): lax.all_gather(own, 'gx', axis=0, tiled=True).astype(jnp.float32)  14.9 us
    pallas_call x2, Pallas kernels, rows_stage(): pl.pallas_call(functools.partial(rows_kernel, len(field)), grid=(slab //...  14.1 us
  transfers between devices with their start and end apart: 22, of which 14 were waited for; matrix products, arithmetic and copies ran while one was open for 4% of the time, Pallas kernels for 15%

profile of v2, /device:TPU:0, one launch (start us, length us, event | category | flops | bytes accessed | tf_op | source)
XLA Modules:
  0.0 491.0 jit_solution(8899118474995148869)
XLA Ops:
  18.1 14.9 %all_gather.17 = bf16[256,128]{1,0:T(8,128)(2,1)S(1)} all-gather(bf16[64,128]{1,0:T(8,128)(2,1)S(1)} %copy.17), channel_id=1, replica_groups=mesh['sta'=2,'gx'=4,'gy'=4] {'gx'}, dimensions={0}, use_global_device_ids=true | all-gather | bytes 81920 | tf_op jit(solution)/shard_map/all_gather | solution.py:270
  36.3 36.2 %all-gather.5.cloned.1.call-done = bf16[128,64,512]{2,1,0:T(8,128)(2,1)} async-done(((bf16[32,64,512]{2,1,0:T(8,128)(2,1)}), bf16[128,64,512]{2,1,0:T(8,128)(2,1)}) %all-gather.5.cloned.1.call-update) | async-done | bytes 8388624 | tf_op jit(solution)/shard_map/all_gather | solution.py:266
  72.5 19.3 %lateral.2 = (bf16[64,32,256]{2,1,0:T(8,128)(2,1)S(1)}, bf16[64,32,256]{2,1,0:T(8,128)(2,1)S(1)}) custom-call(bf16[4,32,64,512]{3,2,1,0:T(8,128)(2,1)} %bitcast.21, bf16[512,256]{1,0:T(8,128)(2,1)S(1)} %get-tuple-element.106.y_high, bf16[512,256]{1,0:T(8,128)(2,1)S(1)} %get-tuple-element.105.y_low, bf16[128,256]{1,0:T(8,128)(2,1)S(1)} %get-tuple-element.110.x_high, ...), custom_call_target="tpu_custom_call" | custom-call | flops 11811160064 | bytes 10485760 | tf_op jit(solution)/shard_map/lateral/pallas_call | solution.py:95
  92.8 39.6 %all-gather.7.cloned.1.call-done = bf16[128,64,512]{2,1,0:T(8,128)(2,1)} async-done(((bf16[32,64,512]{2,1,0:T(8,128)(2,1)}), bf16[128,64,512]{2,1,0:T(8,128)(2,1)}) %all-gather.7.cloned.1.call-update) | async-done | bytes 8388624 | tf_op jit(solution)/shard_map/all_gather | solution.py:266
  132.4 19.1 %lateral.3 = (bf16[64,32,256]{2,1,0:T(8,128)(2,1)S(1)}, bf16[64,32,256]{2,1,0:T(8,128)(2,1)S(1)}) custom-call(bf16[4,32,64,512]{3,2,1,0:T(8,128)(2,1)} %bitcast.22, bf16[512,256]{1,0:T(8,128)(2,1)S(1)} %get-tuple-element.106.y_high, bf16[512,256]{1,0:T(8,128)(2,1)S(1)} %get-tuple-element.105.y_low, bf16[128,256]{1,0:T(8,128)(2,1)S(1)} %get-tuple-element.110.x_high, ...), custom_call_target="tpu_custom_call" | custom-call | flops 11811160064 | bytes 10485760 | tf_op jit(solution)/shard_map/lateral/pallas_call | solution.py:95
  157.1 21.6 %collective-permute-done.refs_2_ = bf16[64,32,256]{2,1,0:T(8,128)(2,1)} collective-permute-done((bf16[64,32,256]{2,1,0:T(8,128)(2,1)S(1)}, bf16[64,32,256]{2,1,0:T(8,128)(2,1)}, u32[]{:S(2)}, u32[]{:S(2)}) %collective-permute-start) | collective-permute-done | bytes 1048608 | tf_op jit(solution)/shard_map/ppermute | solution.py:248
  178.6 21.8 %collective-permute-done.1.refs_3_ = bf16[64,32,256]{2,1,0:T(8,128)(2,1)} collective-permute-done((bf16[64,32,256]{2,1,0:T(8,128)(2,1)S(1)}, bf16[64,32,256]{2,1,0:T(8,128)(2,1)}, u32[]{:S(2)}, u32[]{:S(2)}) %collective-permute-start.1) | collective-permute-done | bytes 1048608 | tf_op jit(solution)/shard_map/ppermute | solution.py:248
  200.4 30.2 %depth.2 = (bf16[32,32,256]{2,1,0:T(8,128)(2,1)S(1)}, bf16[32,32,256]{2,1,0:T(8,128)(2,1)S(1)}, bf16[32,32,256]{2,1,0:T(8,128)(2,1)S(1)}, bf16[32,32,256]{2,1,0:...) custom-call(bf16[512,320]{1,0:T(8,128)(2,1)S(1)} %pad_maximum_fusion, ...), custom_call_target="tpu_custom_call" | custom-call | flops 18253611008 | bytes 16777216 | tf_op jit(solution)/shard_map/depth/pallas_call | solution.py:151
  235.9 30.2 %depth.3 = (bf16[32,32,256]{2,1,0:T(8,128)(2,1)S(1)}, bf16[32,32,256]{2,1,0:T(8,128)(2,1)S(1)}, bf16[32,32,256]{2,1,0:T(8,128)(2,1)S(1)}, bf16[32,32,256]{2,1,0:...) custom-call(bf16[512,320]{1,0:T(8,128)(2,1)S(1)} %pad_maximum_fusion, ...), custom_call_target="tpu_custom_call" | custom-call | flops 18253611008 | bytes 16777216 | tf_op jit(solution)/shard_map/depth/pallas_call | solution.py:151
  271.2 10.0 %collective-permute-start.5 = (bf16[32,32,256]{2,1,0:T(8,128)(2,1)S(1)}, bf16[32,32,256]{2,1,0:T(8,128)(2,1)S(1)}, u32[]{:S(2)}, u32[]{:S(2)}) collective-permute-start(bf16[32,32,256]{2,1,0:T(8,128)(2,1)S(1)} %get-tuple-element.70), channel_id=1, source_target_pairs={{0,4},{4,0},{8,12},{12,8},{1,5},{5,1},{9,13},{13,9},{2,6},{6,2},{1... | collective-permute-start | bytes 1572872 | tf_op jit(solution)/shard_map/ppermute | solution.py:248
  287.4 13.8 %collective-permute-done.5.refs_5_ = bf16[32,32,256]{2,1,0:T(8,128)(2,1)S(1)} collective-permute-done((bf16[32,32,256]{2,1,0:T(8,128)(2,1)S(1)}, bf16[32,32,256]{2,1,0:T(8,128)(2,1)S(1)}, u32[]{:S(2)}, u32[]{:S(2)}) %collective-permute-start.5) | collective-permute-done | bytes 524320 | tf_op jit(solution)/shard_map/ppermute | solution.py:248
  301.2 18.2 %collective-permute-done.6.refs_6_ = bf16[32,32,256]{2,1,0:T(8,128)(2,1)S(1)} collective-permute-done((bf16[32,32,256]{2,1,0:T(8,128)(2,1)S(1)}, bf16[32,32,256]{2,1,0:T(8,128)(2,1)S(1)}, u32[]{:S(2)}, u32[]{:S(2)}) %collective-permute-start.6) | collective-permute-done | bytes 524320 | tf_op jit(solution)/shard_map/ppermute | solution.py:248
  319.4 8.8 %collective-permute-start.8 = (bf16[32,32,256]{2,1,0:T(8,128)(2,1)S(1)}, bf16[32,32,256]{2,1,0:T(8,128)(2,1)S(1)}, u32[]{:S(2)}, u32[]{:S(2)}) collective-permute-start(bf16[32,32,256]{2,1,0:T(8,128)(2,1)S(1)} %get-tuple-element.74), channel_id=1, source_target_pairs={{0,4},{4,0},{8,12},{12,8},{1,5},{5,1},{9,13},{13,9},{2,6},{6,2},{1... | collective-permute-start | bytes 1572872 | tf_op jit(solution)/shard_map/ppermute | solution.py:248
  330.7 7.0 %rows.2 = (bf16[32,64,256]{2,1,0:T(8,128)(2,1)}, bf16[32,64,256]{2,1,0:T(8,128)(2,1)}, bf16[32,64,256]{2,1,0:T(8,128)(2,1)}, bf16[32,64,256]{2,1,0:T(8,128)(2,1)}) custom-call(bf16[32,32,256]{2,1,0:T(8,128)(2,1)S(1)} %get-tuple-element.81.refs_0_, bf16[32,32,256]{2,1,0:T(8,128)(2,1)S(1)} %collective-permute-done.2.refs_1_, ...), custom_call_target="tpu_custom_call" | custom-call | flops 8589934592 | bytes 8388608 | tf_op jit(solution)/shard_map/rows/pallas_call | solution.py:197
  337.8 8.8 %collective-permute-done.8.refs_1_ = bf16[32,32,256]{2,1,0:T(8,128)(2,1)S(1)} collective-permute-done((bf16[32,32,256]{2,1,0:T(8,128)(2,1)S(1)}, bf16[32,32,256]{2,1,0:T(8,128)(2,1)S(1)}, u32[]{:S(2)}, u32[]{:S(2)}) %collective-permute-start.8) | collective-permute-done | bytes 524320 | tf_op jit(solution)/shard_map/ppermute | solution.py:248
  346.5 20.0 %collective-permute-done.9.refs_2_ = bf16[32,32,256]{2,1,0:T(8,128)(2,1)S(1)} collective-permute-done((bf16[32,32,256]{2,1,0:T(8,128)(2,1)S(1)}, bf16[32,32,256]{2,1,0:T(8,128)(2,1)S(1)}, u32[]{:S(2)}, u32[]{:S(2)}) %collective-permute-start.9) | collective-permute-done | bytes 524320 | tf_op jit(solution)/shard_map/ppermute | solution.py:248
  366.5 7.7 %collective-permute-start.11 = (bf16[32,32,256]{2,1,0:T(8,128)(2,1)S(1)}, bf16[32,32,256]{2,1,0:T(8,128)(2,1)S(1)}, u32[]{:S(2)}, u32[]{:S(2)}) collective-permute-start(bf16[32,32,256]{2,1,0:T(8,128)(2,1)S(1)} %get-tuple-element.88), channel_id=1, source_target_pairs={{0,4},{4,0},{8,12},{12,8},{1,5},{5,1},{9,13},{13,9},{2,6},{6,2},{1... | collective-permute-start | bytes 1572872 | tf_op jit(solution)/shard_map/ppermute | solution.py:248
  381.5 9.1 %collective-permute-done.11.refs_5_ = bf16[32,32,256]{2,1,0:T(8,128)(2,1)S(1)} collective-permute-done((bf16[32,32,256]{2,1,0:T(8,128)(2,1)S(1)}, bf16[32,32,256]{2,1,0:T(8,128)(2,1)S(1)}, u32[]{:S(2)}, u32[]{:S(2)}) %collective-permute-start.11) | collective-permute-done | bytes 524320 | tf_op jit(solution)/shard_map/ppermute | solution.py:248
  390.6 22.1 %collective-permute-done.12.refs_6_ = bf16[32,32,256]{2,1,0:T(8,128)(2,1)} collective-permute-done((bf16[32,32,256]{2,1,0:T(8,128)(2,1)}, bf16[32,32,256]{2,1,0:T(8,128)(2,1)}, u32[]{:S(2)}, u32[]{:S(2)}) %collective-permute-start.12) | collective-permute-done | bytes 524320 | tf_op jit(solution)/shard_map/ppermute | solution.py:248
  414.8 7.1 %rows.3 = (bf16[32,64,256]{2,1,0:T(8,128)(2,1)}, bf16[32,64,256]{2,1,0:T(8,128)(2,1)}, bf16[32,64,256]{2,1,0:T(8,128)(2,1)}, bf16[32,64,256]{2,1,0:T(8,128)(2,1)}) custom-call(bf16[32,32,256]{2,1,0:T(8,128)(2,1)S(1)} %copy-done.7, bf16[32,32,256]{2,1,0:T(8,128)(2,1)S(1)} %collective-permute-done.8.refs_1_, ...), custom_call_target="tpu_custom_call" | custom-call | flops 8589934592 | bytes 8388608 | tf_op jit(solution)/shard_map/rows/pallas_call | solution.py:197
  429.8 9.3 %image.2.refs_6_ = f32[64,64,512]{2,1,0:T(8,128)} custom-call(bf16[32,64,256]{2,1,0:T(8,128)(2,1)S(1)} %copy-done.3, bf16[32,64,256]{2,1,0:T(8,128)(2,1)S(1)} %collective-permute-done.17.refs_1_, bf16[32,64,256]{2,1,0:T(8,128)(2,1)S(1)} %collective-permute-done.18.refs_2_, bf16[32,64,256]{2,1,0:T(8,128)(2,1)} %copy-done.14, ...), custom_call_target="tpu_custom_call" | custom-call | flops 8589934592 | bytes 8388608 | tf_op jit(solution)/shard_map/image/pallas_call | solution.py:230
  439.1 13.0 %collective-permute-done.15.refs_2_ = bf16[32,64,256]{2,1,0:T(8,128)(2,1)S(1)} collective-permute-done((bf16[32,64,256]{2,1,0:T(8,128)(2,1)}, bf16[32,64,256]{2,1,0:T(8,128)(2,1)S(1)}, u32[]{:S(2)}, u32[]{:S(2)}) %collective-permute-start.15) | collective-permute-done | bytes 1048608 | tf_op jit(solution)/shard_map/ppermute | solution.py:248
  452.0 21.6 %collective-permute-done.16.refs_3_ = bf16[32,64,256]{2,1,0:T(8,128)(2,1)S(1)} collective-permute-done((bf16[32,64,256]{2,1,0:T(8,128)(2,1)}, bf16[32,64,256]{2,1,0:T(8,128)(2,1)S(1)}, u32[]{:S(2)}, u32[]{:S(2)}) %collective-permute-start.16) | collective-permute-done | bytes 1048608 | tf_op jit(solution)/shard_map/ppermute | solution.py:248
  474.7 9.2 %image.3 = f32[64,64,512]{2,1,0:T(8,128)} custom-call(bf16[32,64,256]{2,1,0:T(8,128)(2,1)S(1)} %copy-done.2, bf16[32,64,256]{2,1,0:T(8,128)(2,1)S(1)} %collective-permute-done.14.refs_1_, bf16[32,64,256]{2,1,0:T(8,128)(2,1)S(1)} %collective-permute-done.15.refs_2_, bf16[32,64,256]{2,1,0:T(8,128)(2,1)} %copy-done.15, ...), custom_call_target="tpu_custom_call", output_to_operand_aliasing={{}: (6, {})} | custom-call | flops 8589934592 | bytes 8388608 | tf_op jit(solution)/shard_map/image/pallas_call | solution.py:230
  (114 shorter events, 58.5 us)
Async XLA Ops:
  6.5 65.9 %all-gather.5.cloned.1.call-start = ((), (), s32[]{:S(2)}) async-start(), calls=%async_computation | async-start | bytes 10485760 | tf_op jit(solution)/shard_map/all_gather | solution.py:266
  11.3 121.1 %all-gather.7.cloned.1.call-start = ((), (), s32[]{:S(2)}) async-start(), calls=%async_computation.1 | async-start | bytes 10485760 | tf_op jit(solution)/shard_map/all_gather | solution.py:266
  152.5 26.1 %collective-permute-start = (bf16[64,32,256]{2,1,0:T(8,128)(2,1)S(1)}, bf16[64,32,256]{2,1,0:T(8,128)(2,1)}, u32[]{:S(2)}, u32[]{:S(2)}) collective-permute-start(bf16[64,32,256]{2,1,0:T(8,128)(2,1)S(1)} %get-tuple-element.54.refs_0_), channel_id=1, source_target_pairs={{0,16},{16,0},{1,17},{17,1},{2,18},{18,2},{3,19},{19,3},{4,20},{20... | collective-permute-start | bytes 3145736 | tf_op jit(solution)/shard_map/ppermute | solution.py:248
  154.0 46.4 %collective-permute-start.1 = (bf16[64,32,256]{2,1,0:T(8,128)(2,1)S(1)}, bf16[64,32,256]{2,1,0:T(8,128)(2,1)}, u32[]{:S(2)}, u32[]{:S(2)}) collective-permute-start(bf16[64,32,256]{2,1,0:T(8,128)(2,1)S(1)} %get-tuple-element.56.refs_1_), channel_id=1, source_target_pairs={{0,16},{16,0},{1,17},{17,1},{2,18},{18,2},{3,19},{19,3},{4,20},{20... | collective-permute-start | bytes 3145736 | tf_op jit(solution)/shard_map/ppermute | solution.py:248
  231.5 34.6 %collective-permute-start.2 = (bf16[32,32,256]{2,1,0:T(8,128)(2,1)S(1)}, bf16[32,32,256]{2,1,0:T(8,128)(2,1)S(1)}, u32[]{:S(2)}, u32[]{:S(2)}) collective-permute-start(bf16[32,32,256]{2,1,0:T(8,128)(2,1)S(1)} %get-tuple-element.67), channel_id=1, source_target_pairs={{0,4},{4,0},{8,12},{12,8},{1,5},{5,1},{9,13},{13,9},{2,6},{6,2},{1... | collective-permute-start | bytes 1572872 | tf_op jit(solution)/shard_map/ppermute | solution.py:248
  233.0 38.2 %collective-permute-start.3 = (bf16[32,32,256]{2,1,0:T(8,128)(2,1)S(1)}, bf16[32,32,256]{2,1,0:T(8,128)(2,1)S(1)}, u32[]{:S(2)}, u32[]{:S(2)}) collective-permute-start(bf16[32,32,256]{2,1,0:T(8,128)(2,1)S(1)} %get-tuple-element.68), channel_id=1, source_target_pairs={{0,8},{4,12},{8,0},{12,4},{1,9},{5,13},{9,1},{13,5},{2,10},{6,14},... | collective-permute-start | bytes 1572872 | tf_op jit(solution)/shard_map/ppermute | solution.py:248
  235.4 92.9 %copy-start.17 = (bf16[32,32,256]{2,1,0:T(8,128)(2,1)S(1)}, bf16[32,32,256]{2,1,0:T(8,128)(2,1)}, u32[]{:S(2)}) copy-start(bf16[32,32,256]{2,1,0:T(8,128)(2,1)} %get-tuple-element.75) | copy-start | bytes 1572868
  235.4 93.8 %copy-start.16 = (bf16[32,32,256]{2,1,0:T(8,128)(2,1)S(1)}, bf16[32,32,256]{2,1,0:T(8,128)(2,1)}, u32[]{:S(2)}) copy-start(bf16[32,32,256]{2,1,0:T(8,128)(2,1)} %get-tuple-element.76) | copy-start | bytes 1572868
  235.4 35.8 %collective-permute-start.4 = (bf16[32,32,256]{2,1,0:T(8,128)(2,1)S(1)}, bf16[32,32,256]{2,1,0:T(8,128)(2,1)S(1)}, u32[]{:S(2)}, u32[]{:S(2)}) collective-permute-start(bf16[32,32,256]{2,1,0:T(8,128)(2,1)S(1)} %get-tuple-element.69), channel_id=1, source_target_pairs={{0,12},{4,8},{8,4},{12,0},{1,13},{5,9},{9,5},{13,1},{2,14},{6,10},... | collective-permute-start | bytes 1572872 | tf_op jit(solution)/shard_map/ppermute | solution.py:248
  271.2 30.0 %collective-permute-start.5 = (bf16[32,32,256]{2,1,0:T(8,128)(2,1)S(1)}, bf16[32,32,256]{2,1,0:T(8,128)(2,1)S(1)}, u32[]{:S(2)}, u32[]{:S(2)}) collective-permute-start(bf16[32,32,256]{2,1,0:T(8,128)(2,1)S(1)} %get-tuple-element.70), channel_id=1, source_target_pairs={{0,4},{4,0},{8,12},{12,8},{1,5},{5,1},{9,13},{13,9},{2,6},{6,2},{1... | collective-permute-start | bytes 1572872 | tf_op jit(solution)/shard_map/ppermute | solution.py:248
  281.2 38.2 %collective-permute-start.6 = (bf16[32,32,256]{2,1,0:T(8,128)(2,1)S(1)}, bf16[32,32,256]{2,1,0:T(8,128)(2,1)S(1)}, u32[]{:S(2)}, u32[]{:S(2)}) collective-permute-start(bf16[32,32,256]{2,1,0:T(8,128)(2,1)S(1)} %get-tuple-element.71), channel_id=1, source_target_pairs={{0,8},{4,12},{8,0},{12,4},{1,9},{5,13},{9,1},{13,5},{2,10},{6,14},... | collective-permute-start | bytes 1572872 | tf_op jit(solution)/shard_map/ppermute | solution.py:248
  282.1 37.3 %collective-permute-start.7 = (bf16[32,32,256]{2,1,0:T(8,128)(2,1)S(1)}, bf16[32,32,256]{2,1,0:T(8,128)(2,1)S(1)}, u32[]{:S(2)}, u32[]{:S(2)}) collective-permute-start(bf16[32,32,256]{2,1,0:T(8,128)(2,1)S(1)} %get-tuple-element.72), channel_id=1, source_target_pairs={{0,12},{4,8},{8,4},{12,0},{1,13},{5,9},{9,5},{13,1},{2,14},{6,10},... | collective-permute-start | bytes 1572872 | tf_op jit(solution)/shard_map/ppermute | solution.py:248
  319.4 27.1 %collective-permute-start.8 = (bf16[32,32,256]{2,1,0:T(8,128)(2,1)S(1)}, bf16[32,32,256]{2,1,0:T(8,128)(2,1)S(1)}, u32[]{:S(2)}, u32[]{:S(2)}) collective-permute-start(bf16[32,32,256]{2,1,0:T(8,128)(2,1)S(1)} %get-tuple-element.74), channel_id=1, source_target_pairs={{0,4},{4,0},{8,12},{12,8},{1,5},{5,1},{9,13},{13,9},{2,6},{6,2},{1... | collective-permute-start | bytes 1572872 | tf_op jit(solution)/shard_map/ppermute | solution.py:248
  328.3 38.2 %collective-permute-start.9 = (bf16[32,32,256]{2,1,0:T(8,128)(2,1)S(1)}, bf16[32,32,256]{2,1,0:T(8,128)(2,1)S(1)}, u32[]{:S(2)}, u32[]{:S(2)}) collective-permute-start(bf16[32,32,256]{2,1,0:T(8,128)(2,1)S(1)} %copy-done.17), channel_id=1, source_target_pairs={{0,8},{4,12},{8,0},{12,4},{1,9},{5,13},{9,1},{13,5},{2,10},{6,14},... | collective-permute-start | bytes 1572872 | tf_op jit(solution)/shard_map/ppermute | solution.py:248
  329.2 37.2 %collective-permute-start.10 = (bf16[32,32,256]{2,1,0:T(8,128)(2,1)S(1)}, bf16[32,32,256]{2,1,0:T(8,128)(2,1)S(1)}, u32[]{:S(2)}, u32[]{:S(2)}) collective-permute-start(bf16[32,32,256]{2,1,0:T(8,128)(2,1)S(1)} %copy-done.16), channel_id=1, source_target_pairs={{0,12},{4,8},{8,4},{12,0},{1,13},{5,9},{9,5},{13,1},{2,14},{6,10},... | collective-permute-start | bytes 1572872 | tf_op jit(solution)/shard_map/ppermute | solution.py:248
  366.5 24.1 %collective-permute-start.11 = (bf16[32,32,256]{2,1,0:T(8,128)(2,1)S(1)}, bf16[32,32,256]{2,1,0:T(8,128)(2,1)S(1)}, u32[]{:S(2)}, u32[]{:S(2)}) collective-permute-start(bf16[32,32,256]{2,1,0:T(8,128)(2,1)S(1)} %get-tuple-element.88), channel_id=1, source_target_pairs={{0,4},{4,0},{8,12},{12,8},{1,5},{5,1},{9,13},{13,9},{2,6},{6,2},{1... | collective-permute-start | bytes 1572872 | tf_op jit(solution)/shard_map/ppermute | solution.py:248
  374.2 38.5 %collective-permute-start.12 = (bf16[32,32,256]{2,1,0:T(8,128)(2,1)}, bf16[32,32,256]{2,1,0:T(8,128)(2,1)}, u32[]{:S(2)}, u32[]{:S(2)}) collective-permute-start(bf16[32,32,256]{2,1,0:T(8,128)(2,1)} %get-tuple-element.89), channel_id=1, source_target_pairs={{0,8},{4,12},{8,0},{12,4},{1,9},{5,13},{9,1},{13,5},{2,10},{6,14},... | collective-permute-start | bytes 1572872 | tf_op jit(solution)/shard_map/ppermute | solution.py:248
  375.1 37.6 %collective-permute-start.13 = (bf16[32,32,256]{2,1,0:T(8,128)(2,1)}, bf16[32,32,256]{2,1,0:T(8,128)(2,1)}, u32[]{:S(2)}, u32[]{:S(2)}) collective-permute-start(bf16[32,32,256]{2,1,0:T(8,128)(2,1)} %get-tuple-element.90), channel_id=1, source_target_pairs={{0,12},{4,8},{8,4},{12,0},{1,13},{5,9},{9,5},{13,1},{2,14},{6,10},... | collective-permute-start | bytes 1572872 | tf_op jit(solution)/shard_map/ppermute | solution.py:248
  379.6 42.9 %collective-permute-start.17 = (bf16[32,64,256]{2,1,0:T(8,128)(2,1)}, bf16[32,64,256]{2,1,0:T(8,128)(2,1)S(1)}, u32[]{:S(2)}, u32[]{:S(2)}) collective-permute-start(bf16[32,64,256]{2,1,0:T(8,128)(2,1)} %get-tuple-element.84), channel_id=1, source_target_pairs={{0,1},{1,0},{2,3},{3,2},{4,5},{5,4},{6,7},{7,6},{8,9},{9,8},{10,11... | collective-permute-start | bytes 3145736 | tf_op jit(solution)/shard_map/ppermute | solution.py:248
  380.9 44.7 %collective-permute-start.18 = (bf16[32,64,256]{2,1,0:T(8,128)(2,1)}, bf16[32,64,256]{2,1,0:T(8,128)(2,1)S(1)}, u32[]{:S(2)}, u32[]{:S(2)}) collective-permute-start(bf16[32,64,256]{2,1,0:T(8,128)(2,1)} %get-tuple-element.85), channel_id=1, source_target_pairs={{0,2},{1,3},{2,0},{3,1},{4,6},{5,7},{6,4},{7,5},{8,10},{9,11},{10,... | collective-permute-start | bytes 3145736 | tf_op jit(solution)/shard_map/ppermute | solution.py:248
  390.6 38.1 %collective-permute-start.19 = (bf16[32,64,256]{2,1,0:T(8,128)(2,1)}, bf16[32,64,256]{2,1,0:T(8,128)(2,1)S(1)}, u32[]{:S(2)}, u32[]{:S(2)}) collective-permute-start(bf16[32,64,256]{2,1,0:T(8,128)(2,1)} %get-tuple-element.86), channel_id=1, source_target_pairs={{0,3},{1,2},{2,1},{3,0},{4,7},{5,6},{6,5},{7,4},{8,11},{9,10},{10,... | collective-permute-start | bytes 3145736 | tf_op jit(solution)/shard_map/ppermute | solution.py:248
  421.9 17.2 %collective-permute-start.14 = (bf16[32,64,256]{2,1,0:T(8,128)(2,1)}, bf16[32,64,256]{2,1,0:T(8,128)(2,1)S(1)}, u32[]{:S(2)}, u32[]{:S(2)}) collective-permute-start(bf16[32,64,256]{2,1,0:T(8,128)(2,1)} %get-tuple-element.92), channel_id=1, source_target_pairs={{0,1},{1,0},{2,3},{3,2},{4,5},{5,4},{6,7},{7,6},{8,9},{9,8},{10,11... | collective-permute-start | bytes 3145736 | tf_op jit(solution)/shard_map/ppermute | solution.py:248
  421.9 30.2 %collective-permute-start.15 = (bf16[32,64,256]{2,1,0:T(8,128)(2,1)}, bf16[32,64,256]{2,1,0:T(8,128)(2,1)S(1)}, u32[]{:S(2)}, u32[]{:S(2)}) collective-permute-start(bf16[32,64,256]{2,1,0:T(8,128)(2,1)} %get-tuple-element.93), channel_id=1, source_target_pairs={{0,2},{1,3},{2,0},{3,1},{4,6},{5,7},{6,4},{7,5},{8,10},{9,11},{10,... | collective-permute-start | bytes 3145736 | tf_op jit(solution)/shard_map/ppermute | solution.py:248
  422.5 51.1 %collective-permute-start.16 = (bf16[32,64,256]{2,1,0:T(8,128)(2,1)}, bf16[32,64,256]{2,1,0:T(8,128)(2,1)S(1)}, u32[]{:S(2)}, u32[]{:S(2)}) collective-permute-start(bf16[32,64,256]{2,1,0:T(8,128)(2,1)} %get-tuple-element.94), channel_id=1, source_target_pairs={{0,3},{1,2},{2,1},{3,0},{4,7},{5,6},{6,5},{7,4},{8,11},{9,10},{10,... | collective-permute-start | bytes 3145736 | tf_op jit(solution)/shard_map/ppermute | solution.py:248
  (19 other events, 351.6 us)
Sparse Core Ops, SparseCore 0:
  11.4 60.9 all-gather.4
  74.0 58.3 all-gather.6
